TPU v7x, 32 devices: a whole 2x2x4 slice. The times are simulated.
32 devices in a mesh: grp: 2 (over x), patch: 16 (over z, y, core).
Axes of the slice: x: 2, y: 2, z: 4, core: 2. Of those that a mesh axis runs over, the one named last changes fastest.
Arguments:
- query: bfloat16 [1536, 5120], P(('grp', 'patch')), parts along dimension 0, may hold values from -128 to 128
- fresh_kv: bfloat16 [2, 1536, 5120], P(None, ('grp', 'patch')), parts along dimension 1, may hold values from -6 to 6
- own_stale: bfloat16 [2, 1536, 5120], P(None, ('grp', 'patch')), parts along dimension 1, may hold values from -6 to 6
- caches: bfloat16 [32, 2, 768, 640], P(('grp', 'patch')), parts along dimension 0, may hold values from -6 to 6
- exponents: int32 [2, 1536, 40], P(None, ('grp', 'patch')), parts along dimension 1, may hold values from -2 to 0
Outputs:
- attended: bfloat16 [1536, 5120], P(('grp', 'patch')), parts along dimension 0
- renewed: bfloat16 [2, 1536, 5120], P(None, ('grp', 'patch')), parts along dimension 1
There are 2 independent parts, one for each index of `grp`. A program takes and returns all parts, laid end to end along the dimension named above; each array names one. Nothing has to cross between parts.
All inputs are finite; a program needn't handle non-finite values.
Results may differ from a plain program's by a relative error of at most 0.0091.
Values may be sent and summed in bfloat16 or wider, within the bound.
A program may use at most 128 MiB of HBM per device.

v0:
```python
import jax
import jax.numpy as jnp
from jax import lax
from jax.sharding import PartitionSpec as P

HG = 8


LIMIT = 8.0


def local(query, fresh_kv, own_stale, caches, exponents):
    rows_own = query.shape[0]
    model_width = query.shape[1]
    devices = lax.axis_size("patch")
    spread = devices // HG
    sub_rows = rows_own // spread
    position = lax.axis_index("patch")
    head_group = position // spread
    head_count = exponents.shape[2]
    head_dim = model_width // head_count
    group_cols = model_width // HG
    group_heads = head_count // HG
    residual = (fresh_kv.astype(jnp.float32) - own_stale.astype(jnp.float32)).reshape(
        2, rows_own, head_count, head_dim
    )
    exponent_f = exponents.astype(jnp.float32)[..., None]
    coded = jnp.clip(residual * jnp.exp2(-exponent_f), -LIMIT, LIMIT).astype(jnp.bfloat16)
    decoded = (
        (coded.astype(jnp.float32) * jnp.exp2(exponent_f))
        .astype(jnp.bfloat16)
        .reshape(2, rows_own, model_width)
    )
    renewed = (own_stale.astype(jnp.float32) + decoded.astype(jnp.float32)).astype(jnp.bfloat16)
    query_pieces = (
        query.reshape(spread, sub_rows, HG, group_cols)
        .transpose(2, 0, 1, 3)
        .reshape(devices, sub_rows, group_cols)
    )
    arrived_queries = lax.all_to_all(query_pieces, "patch", split_axis=0, concat_axis=1, tiled=True)
    query_rows = arrived_queries.reshape(devices * sub_rows, group_cols)
    by_group = decoded.reshape(2, rows_own, HG, group_cols)
    pieces = by_group.transpose(2, 0, 1, 3)
    pieces = jnp.broadcast_to(pieces[:, None], (HG, spread, 2, rows_own, group_cols)).reshape(
        devices, 2, rows_own, group_cols
    )
    arrived = lax.all_to_all(pieces, "patch", split_axis=0, concat_axis=2, tiled=True)
    arrived = arrived.reshape(2, devices * rows_own, group_cols)
    stored = (caches[0].astype(jnp.float32) + arrived.astype(jnp.float32)).astype(jnp.bfloat16)
    local_rows = lax.dynamic_slice_in_dim(fresh_kv, head_group * group_cols, group_cols, 2)
    stored = lax.dynamic_update_slice_in_dim(stored, local_rows, position * rows_own, 1)
    key_rows = stored[0]
    value_rows = stored[1]
    scale = head_dim ** (-0.5)

    def head_attention(head_number):
        start = head_number * head_dim
        query_head = lax.dynamic_slice_in_dim(query_rows, start, head_dim, 1)
        key_head = lax.dynamic_slice_in_dim(key_rows, start, head_dim, 1)
        value_head = lax.dynamic_slice_in_dim(value_rows, start, head_dim, 1)
        scores = (
            lax.dot_general(
                query_head, key_head, (((1,), (1,)), ((), ())), preferred_element_type=jnp.float32
            )
            * scale
        )
        peak = jnp.max(scores, axis=-1, keepdims=True)
        raised = jnp.exp(scores - peak)
        weights = (raised / jnp.sum(raised, axis=-1, keepdims=True)).astype(jnp.bfloat16)
        return jnp.dot(weights, value_head, preferred_element_type=jnp.float32).astype(jnp.bfloat16)

    per_head = lax.map(head_attention, jnp.arange(group_heads, dtype=jnp.int32))
    answer_pieces = per_head.transpose(1, 0, 2).reshape(devices, sub_rows, group_cols)
    returned = lax.all_to_all(answer_pieces, "patch", split_axis=0, concat_axis=0, tiled=True)
    attended = (
        returned.reshape(HG, spread, sub_rows, group_cols)
        .transpose(1, 2, 0, 3)
        .reshape(rows_own, model_width)
    )
    return (attended, renewed)


def solution(mesh):
    return jax.shard_map(
        local,
        mesh=mesh,
        in_specs=(
            P(("grp", "patch"), None),
            P(None, ("grp", "patch"), None),
            P(None, ("grp", "patch"), None),
            P(("grp", "patch"), None, None, None),
            P(None, ("grp", "patch"), None),
        ),
        out_specs=(P(("grp", "patch"), None), P(None, ("grp", "patch"), None)),
        check_vma=False,
    )
```

profile of v0, /device:TPU:0, one launch (start us, length us, event | category | flops | bytes accessed | tf_op | source)
XLA Modules:
  0.0 120.0 jit_solution(12837081751336236730)
XLA Ops:
  0.6 0.8 multiply_exponential_fusion.1
  1.5 0.6 mul.47
  2.1 1.6 %mul.55 = f32[2,48,5120]{2,1,0:T(8,128)} reshape(f32[2,48,40,128]{3,2,1,0:T(8,128)S(1)} %mul.47) | data formatting | bytes 3932160 | tf_op jit(solution)/shard_map/mul | solution.py:28
  3.7 1.7 %mul.48 = f32[2,48,8,640]{3,2,1,0:T(8,128)} reshape(f32[2,48,40,128]{3,2,1,0:T(8,128)S(1)} %mul.47) | data formatting | bytes 3932160 | tf_op jit(solution)/shard_map/mul | solution.py:28
  5.4 0.6 mul.50
  6.0 1.6 %mul.57 = f32[2,48,5120]{2,1,0:T(8,128)} reshape(f32[2,48,40,128]{3,2,1,0:T(8,128)S(1)} %mul.50) | data formatting | bytes 3932160 | tf_op jit(solution)/shard_map/mul | solution.py:30
  7.6 1.7 %mul.51 = f32[2,48,8,640]{3,2,1,0:T(8,128)} reshape(f32[2,48,40,128]{3,2,1,0:T(8,128)S(1)} %mul.50) | data formatting | bytes 3932160 | tf_op jit(solution)/shard_map/mul | solution.py:30
  9.3 3.9 %fusion.9 = (bf16[2,48,5120]{2,1,0:T(8,128)(2,1)}, f32[2,48,5120]{2,1,0:T(8,128)S(1)}) fusion(bf16[2,48,5120]{2,1,0:T(8,128)(2,1)} %param.9, f32[2,48,5120]{2,1,0:T(8,128)} %mul.57, f32[2,48,5120]{2,1,0:T(8,128)} %mul.55, bf16[2,48,5120]{2,1,0:T(8,128)(2,1)S(1)} %copy-done.3), kind=kLoop, calls=%fused_computation.16 | loop fusion | flops 5898240 | bytes 8847360 | tf_op jit(solution)/shard_map/convert_element_type | solution.py:34
  13.5 1.2 copy-done
  14.7 0.6 copy-done.1
  15.8 1.5 %broadcast_in_dim.8 = bf16[8,2,2,48,640]{4,3,2,1,0:T(8,128)(2,1)} broadcast(bf16[8,2,48,640]{3,2,1,0:T(8,128)(2,1)S(1)} %copy.31), dimensions={0,2,3,4} | broadcast | bytes 2949120 | tf_op jit(solution)/shard_map/broadcast_in_dim | solution.py:44
  17.3 7.4 %all-to-all-start.1 = ((bf16[16,2,48,640]{3,2,1,0:T(8,128)(2,1)}), bf16[16,2,48,640]{3,2,1,0:T(8,128)(2,1)S(1)}, u32[]{:S(2)}, u32[]{:S(2)}) async-start(bf16[16,2,48,640]{3,2,1,0:T(8,128)(2,1)} %bitcast.62), calls=%async_computation.1 | async-start | bytes 3932160 | tf_op jit(solution)/shard_map/all_to_all | solution.py:47
  24.7 1.1 copy.35
  25.9 0.8 copy.28
  26.7 36.8 %all-to-all-done.1 = bf16[16,2,48,640]{3,2,1,0:T(8,128)(2,1)S(1)} async-done(((bf16[16,2,48,640]{3,2,1,0:T(8,128)(2,1)}), bf16[16,2,48,640]{3,2,1,0:T(8,128)(2,1)S(1)}, u32[]{:S(2)}, u32[]{:S(2)}) %all-to-all-start.1) | async-done | bytes 1966112 | tf_op jit(solution)/shard_map/all_to_all | solution.py:47
  63.5 10.7 %all-to-all-start = ((bf16[16,24,640]{2,1,0:T(8,128)(2,1)}), bf16[16,24,640]{2,1,0:T(8,128)(2,1)S(1)}, u32[]{:S(2)}, u32[]{:S(2)}) async-start(bf16[16,24,640]{2,1,0:T(8,128)(2,1)} %bitcast.3), calls=%async_computation | async-start | bytes 983040 | tf_op jit(solution)/shard_map/all_to_all | solution.py:40
  74.5 1.3 %copy-done.2 = bf16[1,2,768,640]{3,2,1,0:T(8,128)(2,1)S(1)} copy-done((bf16[1,2,768,640]{3,2,1,0:T(8,128)(2,1)S(1)}, bf16[1,2,768,640]{3,2,1,0:T(8,128)(2,1)}, u32[]{:S(2)}) %copy-start.2) | copy-done | bytes 1966104
  76.4 11.5 %all-to-all-done = bf16[16,24,640]{2,1,0:T(8,128)(2,1)S(1)} async-done(((bf16[16,24,640]{2,1,0:T(8,128)(2,1)}), bf16[16,24,640]{2,1,0:T(8,128)(2,1)S(1)}, u32[]{:S(2)}, u32[]{:S(2)}) %all-to-all-start) | async-done | bytes 491552 | tf_op jit(solution)/shard_map/all_to_all | solution.py:40
  88.0 12.4 %while.10 = (s32[]{:T(128)}, bf16[5,384,128]{2,1,0:T(8,128)(2,1)S(1)}, s32[5]{0:T(128)S(1)}, bf16[384,640]{1,0:T(8,128)(2,1)S(1)}, bf16[768,640]{1,0:T(8,128)(2,...) while((s32[]{:T(128)}, bf16[5,384,128]{2,1,0:T(8,128)(2,1)S(1)}, ...), condition=%wide.region_3.4_spmd, body=%wide.region_0.3_spmd.sunk | while | flops 153107712 | bytes 4138663 | solution.py:72
  88.0 0.6 dynamic_slice.35
  90.0 0.5 fusion.21
  90.5 0.6 dynamic_slice.35
  92.5 0.5 fusion.21
  93.0 0.6 dynamic_slice.35
  95.0 0.5 fusion.21
  95.5 0.6 dynamic_slice.35
  97.5 0.5 fusion.21
  97.9 0.6 dynamic_slice.35
  99.9 0.5 fusion.21
  100.8 0.6 reshape.63
  101.4 17.7 %all_to_all.23 = bf16[16,24,640]{2,1,0:T(8,128)(2,1)S(1)} all-to-all(bf16[16,24,640]{2,1,0:T(8,128)(2,1)S(1)} %reshape.63), channel_id=1, replica_groups=mesh['grp'=2,'patch'=16] {'patch'}, dimensions={0} | all-to-all | bytes 983040 | tf_op jit(solution)/shard_map/all_to_all | solution.py:74
  119.1 0.8 copy.37
  (31 shorter events, 6.2 us)
Async XLA Ops:
  7.6 1.7 %copy-start.3 = (bf16[2,48,5120]{2,1,0:T(8,128)(2,1)S(1)}, bf16[2,48,5120]{2,1,0:T(8,128)(2,1)}, u32[]{:S(2)}) copy-start(bf16[2,48,5120]{2,1,0:T(8,128)(2,1)} %param.8) | copy-start | bytes 2949124
  13.2 1.5 %copy-start = (f32[2,48,8,640]{3,2,1,0:T(8,128)S(1)}, f32[2,48,8,640]{3,2,1,0:T(8,128)}, u32[]{:S(2)}) copy-start(f32[2,48,8,640]{3,2,1,0:T(8,128)} %mul.48) | copy-start | bytes 5898244
  13.2 2.1 %copy-start.1 = (f32[2,48,8,640]{3,2,1,0:T(8,128)S(1)}, f32[2,48,8,640]{3,2,1,0:T(8,128)}, u32[]{:S(2)}) copy-start(f32[2,48,8,640]{3,2,1,0:T(8,128)} %mul.51) | copy-start | bytes 5898244
  17.3 46.2 %all-to-all-start.1 = ((bf16[16,2,48,640]{3,2,1,0:T(8,128)(2,1)}), bf16[16,2,48,640]{3,2,1,0:T(8,128)(2,1)S(1)}, u32[]{:S(2)}, u32[]{:S(2)}) async-start(bf16[16,2,48,640]{3,2,1,0:T(8,128)(2,1)} %bitcast.62), calls=%async_computation.1 | async-start | bytes 3932160 | tf_op jit(solution)/shard_map/all_to_all | solution.py:47
  63.5 24.5 %all-to-all-start = ((bf16[16,24,640]{2,1,0:T(8,128)(2,1)}), bf16[16,24,640]{2,1,0:T(8,128)(2,1)S(1)}, u32[]{:S(2)}, u32[]{:S(2)}) async-start(bf16[16,24,640]{2,1,0:T(8,128)(2,1)} %bitcast.3), calls=%async_computation | async-start | bytes 983040 | tf_op jit(solution)/shard_map/all_to_all | solution.py:40
  74.2 1.5 %copy-start.2 = (bf16[1,2,768,640]{3,2,1,0:T(8,128)(2,1)S(1)}, bf16[1,2,768,640]{3,2,1,0:T(8,128)(2,1)}, u32[]{:S(2)}) copy-start(bf16[1,2,768,640]{3,2,1,0:T(8,128)(2,1)} %param.10) | copy-start | bytes 5898244
  76.3 11.7 %copy-start.4 = (bf16[5,384,128]{2,1,0:T(8,128)(2,1)S(1)}, bf16[5,384,128]{2,1,0:T(8,128)(2,1)}, u32[]{:S(2)}) copy-start(bf16[5,384,128]{2,1,0:T(8,128)(2,1)} %custom-call) | copy-start | bytes 1474564
where the time goes:
time: 120 us
  waiting for transfers between devices  48.4 us (40%)
  local copies, waits for them, and re-layouts  19.8 us (16%)
  starting transfers between devices  18.1 us (15%)
  blocking collectives  17.7 us (15%)
  other arithmetic  7.56 us (6%)
  matrix products  4.37 us (4%)
  loops' own time  3.36 us (3%)
    all_to_all x1, waiting for transfers between devices, local(): lax.all_to_all(pieces, 'patch', split_axis=0, concat_axis=2, tiled=True)  36.8 us
    all_to_all x1, blocking collectives, local(): lax.all_to_all(answer_pieces, 'patch', split_axis=0, concat_axis=0, tiled...  17.7 us
    all_to_all x1, waiting for transfers between devices, local(): lax.all_to_all(query_pieces, 'patch', split_axis=0, concat_axis=1, tiled=...  11.5 us
    all_to_all x1, starting transfers between devices, local(): lax.all_to_all(query_pieces, 'patch', split_axis=0, concat_axis=1, tiled=...  10.7 us
    all_to_all x1, starting transfers between devices, local(): lax.all_to_all(pieces, 'patch', split_axis=0, concat_axis=2, tiled=True)  7.39 us
    unnamed x13, local copies, waits for them, and re-layouts  5.34 us
    convert_element_type x1, other arithmetic, local(): (own_stale.astype(jnp.float32) + decoded.astype(jnp.float32)).astype(jnp....  3.9 us
    mul x3, local copies, waits for them, and re-layouts, local(): residual * jnp.exp2(-exponent_f)  3.86 us
  transfers between devices with their start and end apart: 2, of which 2 were waited for; matrix products, arithmetic and copies ran while one was open for 2% of the time, Pallas kernels for 0%

commit v1 on v0

v1 whole, which is shorter than its diff:
```python
import functools
import math

import jax
import jax.numpy as jnp
from jax import lax
from jax.experimental import pallas as pl
from jax.experimental.pallas import tpu as pltpu
from jax.sharding import PartitionSpec as P

HG = 8
LIMIT = 8.0
MESH = pl.DeviceIdType.MESH
ORDER = (4, 6, 5, 7, 2, 3, 1, 0)


def round_up(value, step):
    return -(-value // step) * step


def partner_group(group, k):
    total = 0
    for b in range(HG.bit_length() - 1):
        bit = lax.rem(lax.div(group, 1 << b), 2)
        total = total + (1 << b) * ((1 - bit) if (k >> b) & 1 else bit)
    return total


def loop(low, high, body):
    if high - low <= 2:
        for i in range(low, high):
            body(i)
    else:

        def step(i, carry):
            body(i)
            return carry

        lax.fori_loop(low, high, step, 0)


def kernel(
    sizes, query, fresh, stale, caches, exps, attended, renewed,
    q_v, f_v, s_v, c_v, e_v, lim, dec, att, ren, keys, values,
    qsend0, qsend1, qsend2, qgot0, qgot1, qgot2, osend0, osend1, osend2, ogot0, ogot1, ogot2,
    arrived, in_sem, out_sem, kv_send, kv_recv, fw_send, q_send, q_recv, o_send, o_recv,
):
    n, spread, rows, sub, unit, head, group_heads, stages = sizes
    cols = group_heads * head
    qsend, qgot = (qsend0, qsend1, qsend2), (qgot0, qgot1, qgot2)
    osend, ogot = (osend0, osend1, osend2), (ogot0, ogot1, ogot2)
    me = lax.axis_index("patch")
    group, member = lax.div(me, spread), lax.rem(me, spread)
    my_rows = pl.ds(pl.multiple_of(me * rows, 16), rows)

    loads = [
        pltpu.make_async_copy(a, b, in_sem.at[i])
        for i, (a, b) in enumerate(
            ((exps, e_v), (fresh, f_v), (stale, s_v), (query, q_v), (caches, c_v))
        )
    ]
    for load in loads:
        load.start()

    barrier = pltpu.get_barrier_semaphore()

    def greet(k):
        pl.semaphore_signal(
            barrier, inc=1, device_id={"patch": lax.rem(me + k, n)}, device_id_type=MESH
        )

    loop(1, n, greet)

    def remote(src, dst, send_sem, recv_sem, device):
        return pltpu.make_async_remote_copy(
            src_ref=src, dst_ref=dst, send_sem=send_sem, recv_sem=recv_sem,
            device_id={"patch": device}, device_id_type=MESH,
        )

    def slab_rows(p):
        return pl.ds(pl.multiple_of(p * rows, 16), rows)

    def landed(s, p):
        first, count = stages[s]
        return arrived.at[pl.ds(first, count), :, slab_rows(p), :]

    def kv_copy(s, go):
        first, count = stages[s]
        return remote(
            dec.at[go, pl.ds(first, count)], landed(s, me),
            kv_send.at[s, go], kv_recv.at[s, me], go * spread + member,
        )

    def forward_copy(s, p, t):
        return remote(
            landed(s, p), landed(s, p),
            fw_send.at[s, lax.div(p, spread), t], kv_recv.at[s, p], group * spread + t,
        )

    def q_copy(s, d):
        return remote(qsend[s].at[d], qgot[s].at[me], q_send.at[s, d], q_recv.at[s, me], d)

    def o_copy(s, p):
        return remote(osend[s].at[p], ogot[s].at[me], o_send.at[s, p], o_recv.at[s, me], p)

    def spread_rows(x):
        if unit == sub:
            return x
        out = lax.broadcasted_iota(jnp.int32, (spread * unit, rows), 0)
        src = lax.broadcasted_iota(jnp.int32, (spread * unit, rows), 1)
        pick = (out // unit * sub + out % unit == src) & (out % unit < sub)
        return jnp.dot(
            pick.astype(jnp.bfloat16), x.astype(jnp.bfloat16), preferred_element_type=jnp.float32
        )

    def join_rows(x):
        if unit == sub:
            return x
        out = lax.broadcasted_iota(jnp.int32, (rows, spread * unit), 0)
        src = lax.broadcasted_iota(jnp.int32, (rows, spread * unit), 1)
        pick = out // sub * unit + out % sub == src
        return jnp.dot(
            pick.astype(jnp.bfloat16), x.astype(jnp.bfloat16), preferred_element_type=jnp.float32
        )

    loads[0].wait()
    head_count = e_v.shape[2]
    lim[...] = (LIMIT * jnp.exp2(e_v[...].astype(jnp.float32))).reshape(2 * rows, head_count).astype(
        jnp.bfloat16
    )
    for load in loads[1:4]:
        load.wait()

    def prepare(s, go):
        first, count = stages[s]
        width = count * head
        start = pl.multiple_of(go * cols + first * head, 128)
        window = pl.ds(start, width)
        which = lax.broadcasted_iota(jnp.int32, (head_count, width), 0)
        column = lax.broadcasted_iota(jnp.int32, (head_count, width), 1)
        one_hot = (which == go * group_heads + first + column // head).astype(jnp.bfloat16)
        limit = jnp.dot(lim[...], one_hot, preferred_element_type=jnp.float32)
        limit = limit.reshape(2, rows, width)
        old = s_v[:, :, window].astype(jnp.float32)
        residual = f_v[:, :, window].astype(jnp.float32) - old
        decoded = jnp.clip(residual, -limit, limit).astype(jnp.bfloat16)
        for j in range(count):
            dec[go, first + j] = decoded[:, :, j * head : (j + 1) * head]
        ren[:, :, window] = (old + decoded.astype(jnp.float32)).astype(jnp.bfloat16)
        block = spread_rows(q_v[:, window].astype(jnp.float32))
        for t in range(spread):
            parts = [
                block[t * unit : (t + 1) * unit, j * head : (j + 1) * head] for j in range(count)
            ]
            spare = qsend[s].shape[1] - count * unit
            if spare:
                parts.append(jnp.zeros((spare, head), jnp.float32))
            qsend[s][go * spread + t] = jnp.concatenate(parts, axis=0).astype(jnp.bfloat16)

    for s in range(len(stages)):
        first, count = stages[s]
        for k in ORDER:
            go = partner_group(group, k)
            prepare(s, go)
            if s == 0 and k == ORDER[0]:
                pl.semaphore_wait(barrier, n - 1)
            if k:
                kv_copy(s, go).start()
                loop(0, spread, lambda t: q_copy(s, go * spread + t).start())
            else:
                arrived[pl.ds(first, count), :, my_rows, :] = dec[group, pl.ds(first, count)]
                qgot[s][me] = qsend[s][me]

                def to_sibling(t):
                    @pl.when(t != member)
                    def _():
                        forward_copy(s, me, t).start()
                        q_copy(s, group * spread + t).start()

                loop(0, spread, to_sibling)

    write_renewed = pltpu.make_async_copy(ren, renewed, out_sem.at[0])
    write_renewed.start()
    loads[4].wait()

    def unpack(s):
        first, count = stages[s]

        def one_group(g):
            def arrive(t):
                @pl.when(g * spread + t != me)
                def _():
                    p = g * spread + t
                    remote(
                        osend[s].at[p], ogot[s].at[p], o_send.at[s, p], o_recv.at[s, p], p
                    ).wait_recv()

            loop(0, spread, arrive)
            got = ogot[s][pl.ds(g * spread, spread)].astype(jnp.float32)
            for j in range(count):
                piece = got[:, j * unit : (j + 1) * unit, :].reshape(spread * unit, head)
                start = pl.multiple_of(g * cols + (first + j) * head, 128)
                att[:, pl.ds(start, head)] = join_rows(piece).astype(jnp.bfloat16)

        loop(0, HG, one_group)

    scale = head ** (-0.5) * math.log2(math.e)
    chunk = 8
    for s in range(len(stages)):
        first, count = stages[s]
        for k in ORDER[:-1]:
            p = partner_group(group, k) * spread + member
            forward_copy(s, p, 0).wait_recv()

            def pass_on(t):
                @pl.when(t != member)
                def _():
                    forward_copy(s, p, t).start()

            loop(0, spread, pass_on)

        def arrive_q(k):
            p = lax.rem(me + k, n)
            remote(qsend[s].at[p], qgot[s].at[p], q_send.at[s, p], q_recv.at[s, p], p).wait_recv()

        loop(1, n, arrive_q)

        def arrive_kv(t):
            @pl.when(t != member)
            def _():
                def one(g):
                    forward_copy(s, g * spread + t, 0).wait_recv()

                loop(0, HG, one)

        loop(0, spread, arrive_kv)

        for j in range(count):
            columns = pl.ds((first + j) * head, head)
            mine = pl.ds(pl.multiple_of(group * cols + (first + j) * head, 128), head)
            for which, store in ((0, keys), (1, values)):
                store[j] = (
                    c_v[0, which, :, columns].astype(jnp.float32)
                    + arrived[first + j, which].astype(jnp.float32)
                ).astype(jnp.bfloat16)
                store[j, my_rows, :] = f_v[which, :, mine]

        for c0 in range(0, n, chunk):
            block = qgot[s][c0 : c0 + chunk].astype(jnp.float32)
            outs = []
            for j in range(count):
                q = block[:, j * unit : (j + 1) * unit, :].reshape(chunk * unit, head)
                scores = lax.dot_general(
                    q.astype(jnp.bfloat16), keys[j], (((1,), (1,)), ((), ())),
                    preferred_element_type=jnp.float32,
                )
                peak = jnp.max(scores, axis=-1, keepdims=True)
                raised = jnp.exp2((scores - peak) * scale)
                total = jnp.sum(raised, axis=-1, keepdims=True)
                mixed = jnp.dot(
                    raised.astype(jnp.bfloat16), values[j], preferred_element_type=jnp.float32
                )
                outs.append((mixed / total).reshape(chunk, unit, head))
            spare = osend[s].shape[1] - count * unit
            if spare:
                outs.append(jnp.zeros((chunk, spare, head), jnp.float32))
            osend[s][c0 : c0 + chunk] = jnp.concatenate(outs, axis=1).astype(jnp.bfloat16)

            def give_back(i):
                p = c0 + i

                @pl.when(p != me)
                def _():
                    o_copy(s, p).start()

                @pl.when(p == me)
                def _():
                    ogot[s][me] = osend[s][me]

            loop(0, chunk, give_back)

    for s in range(len(stages)):
        unpack(s)
    write_attended = pltpu.make_async_copy(att, attended, out_sem.at[1])
    write_attended.start()

    for s in range(len(stages)):

        def left(k):
            p = lax.rem(me + k, n)
            q_copy(s, p).wait_send()
            o_copy(s, p).wait_send()

        loop(1, n, left)
        for k in ORDER[:-1]:
            kv_copy(s, partner_group(group, k)).wait_send()

        def left_sibling(t):
            @pl.when(t != member)
            def _():
                def one(g):
                    forward_copy(s, g * spread + member, t).wait_send()

                loop(0, HG, one)

        loop(0, spread, left_sibling)
    write_renewed.wait()
    write_attended.wait()


def local(query, fresh_kv, own_stale, caches, exponents):
    rows, width = query.shape
    n = lax.axis_size("patch")
    spread = n // HG
    sub = rows // spread
    head = width // exponents.shape[2]
    group_heads = exponents.shape[2] // HG
    cols = width // HG
    unit = round_up(sub, 8)
    cuts = (0, 2, 4, group_heads)
    stages = tuple((a, b - a) for a, b in zip(cuts[:-1], cuts[1:]))
    tokens = caches.shape[2]
    most = max(count for _, count in stages)
    bf16 = jnp.bfloat16
    packs = [(n, round_up(count * unit, 16), head) for _, count in stages]
    dma = pltpu.SemaphoreType.DMA
    ns = len(stages)
    scratch = (
        [
            pltpu.VMEM(query.shape, bf16),
            pltpu.VMEM(fresh_kv.shape, bf16),
            pltpu.VMEM(own_stale.shape, bf16),
            pltpu.VMEM(caches.shape, bf16),
            pltpu.VMEM(exponents.shape, jnp.int32),
            pltpu.VMEM((2 * rows, exponents.shape[2]), bf16),
            pltpu.VMEM((HG, group_heads, 2, rows, head), bf16),
            pltpu.VMEM(query.shape, bf16),
            pltpu.VMEM(fresh_kv.shape, bf16),
            pltpu.VMEM((most, tokens, head), bf16),
            pltpu.VMEM((most, tokens, head), bf16),
        ]
        + [pltpu.VMEM(pack, bf16) for _ in range(4) for pack in packs]
        + [
            pltpu.VMEM((group_heads, 2, tokens, head), bf16),
            dma((5,)),
            dma((2,)),
            dma((ns, HG)),
            dma((ns, n)),
            dma((ns, HG, spread)),
            dma((ns, n)),
            dma((ns, n)),
            dma((ns, n)),
            dma((ns, n)),
        ]
    )
    sizes = (n, spread, rows, sub, unit, head, group_heads, stages)
    anywhere = pl.BlockSpec(memory_space=pl.ANY)
    return pl.pallas_call(
        functools.partial(kernel, sizes),
        out_shape=(
            jax.ShapeDtypeStruct(query.shape, bf16),
            jax.ShapeDtypeStruct(fresh_kv.shape, bf16),
        ),
        in_specs=[anywhere] * 5,
        out_specs=(anywhere, anywhere),
        scratch_shapes=scratch,
        compiler_params=pltpu.CompilerParams(
            collective_id=0, has_side_effects=True, vmem_limit_bytes=48 * 1024 * 1024
        ),
    )(query, fresh_kv, own_stale, caches, exponents)


def solution(mesh):
    return jax.shard_map(
        local,
        mesh=mesh,
        in_specs=(
            P(("grp", "patch"), None),
            P(None, ("grp", "patch"), None),
            P(None, ("grp", "patch"), None),
            P(("grp", "patch"), None, None, None),
            P(None, ("grp", "patch"), None),
        ),
        out_specs=(P(("grp", "patch"), None), P(None, ("grp", "patch"), None)),
        check_vma=False,
    )
```

time: 120 us -> 64.3 us (0.54)
  Pallas kernels: 0 us -> 55.8 us
  waiting for transfers between devices: 48.4 us -> 0 us
  starting transfers between devices: 18.1 us -> 0 us
  blocking collectives: 17.7 us -> 0 us
  local copies, waits for them, and re-layouts: 19.8 us -> 7.56 us
  other arithmetic: 7.56 us -> 0 us
  matrix products: 4.37 us -> 0 us
  loops' own time: 3.36 us -> 0 us
    pallas_call x0 -> x1, Pallas kernels: none -> 55.8 us  [local(): pl.pallas_call(functools.partial(kernel, sizes), out_shape=(jax.ShapeDtyp...]
    all_to_all x2 -> x0, waiting for transfers between devices: 48.4 us -> none  [the longest x1 36.8 us: local(): lax.all_to_all(pieces, 'patch', split_axis=0, concat_axis=2, tiled=True)]
    all_to_all x2 -> x0, starting transfers between devices: 18.1 us -> none  [the longest x1 10.7 us: local(): lax.all_to_all(query_pieces, 'patch', split_axis=0, concat_axis=1, tiled=...]
    all_to_all x1 -> x0, blocking collectives: 17.7 us -> none  [local(): lax.all_to_all(answer_pieces, 'patch', split_axis=0, concat_axis=0, tiled...]
    mul x6 -> x0, local copies, waits for them, and re-layouts: 7.66 us -> none  [the longest x3 3.86 us: local(): residual * jnp.exp2(-exponent_f)]
    convert_element_type x3 -> x0, other arithmetic: 4.61 us -> none  [the longest x1 3.9 us: local(): (own_stale.astype(jnp.float32) + decoded.astype(jnp.float32)).astype(jnp....]
    dot_general x10 -> x0, matrix products: 4.37 us -> none  [the longest x5 2.36 us: head_attention(): jnp.dot(weights, value_head, preferred_element_type=jnp.float32)]
    another operation x1 -> x0, loops' own time: 3.36 us -> none  [local(): per_head = lax.map(head_attention, jnp.arange(group_heads, dtype=jnp.int32))]
  transfers between devices with their start and end apart: 2 -> 0, of which waited for: 2 -> 0; matrix products, arithmetic and copies ran while one was open for 2% -> 0% of each run, Pallas kernels for 0% -> 0%
where the time goes in v1:
time: 64.3 us; the launch traced here: 64 us
  Pallas kernels  55.8 us (87%)
  local copies, waits for them, and re-layouts  7.56 us (12%)
    pallas_call x1, Pallas kernels, local(): pl.pallas_call(functools.partial(kernel, sizes), out_shape=(jax.ShapeDtyp...  55.8 us
    unnamed x11, local copies, waits for them, and re-layouts  7.56 us

profile of v1, /device:TPU:0, one launch (start us, length us, event | category | flops | bytes accessed | tf_op | source)
XLA Modules:
  0.0 64.0 jit_solution(1035491519546840495)
XLA Ops:
  0.6 0.9 %copy.7.exps = s32[2,48,40]{2,1,0:T(8,128)S(1)} copy(s32[2,48,40]{1,2,0:T(8,128)} %param.9) | data formatting | bytes 30720 | tf_op args[4]
  1.5 0.0 copy-start
  1.5 1.5 %copy-done = bf16[1,2,768,640]{3,2,1,0:T(8,128)(2,1)S(1)} copy-done((bf16[1,2,768,640]{3,2,1,0:T(8,128)(2,1)S(1)}, bf16[1,2,768,640]{3,2,1,0:T(8,128)(2,1)}, u32[]{:S(2)}) %copy-start) | copy-done | bytes 1966104
  3.0 0.0 copy-start.1
  3.0 1.2 %copy-done.1 = bf16[2,48,5120]{2,1,0:T(8,128)(2,1)S(1)} copy-done((bf16[2,48,5120]{2,1,0:T(8,128)(2,1)S(1)}, bf16[2,48,5120]{2,1,0:T(8,128)(2,1)}, u32[]{:S(2)}) %copy-start.1) | copy-done | bytes 983064
  4.2 0.0 copy-start.2
  4.2 1.2 %copy-done.2 = bf16[2,48,5120]{2,1,0:T(8,128)(2,1)S(1)} copy-done((bf16[2,48,5120]{2,1,0:T(8,128)(2,1)S(1)}, bf16[2,48,5120]{2,1,0:T(8,128)(2,1)}, u32[]{:S(2)}) %copy-start.2) | copy-done | bytes 983064
  5.4 0.0 copy-start.3
  5.4 1.0 %copy-done.3 = bf16[48,5120]{1,0:T(8,128)(2,1)S(1)} copy-done((bf16[48,5120]{1,0:T(8,128)(2,1)S(1)}, bf16[48,5120]{1,0:T(8,128)(2,1)}, u32[]{:S(2)}) %copy-start.3) | copy-done | bytes 491544
  6.5 55.8 %shard_map.68 = (bf16[48,5120]{1,0:T(8,128)(2,1)S(1)}, bf16[2,48,5120]{2,1,0:T(8,128)(2,1)S(1)}) custom-call(bf16[48,5120]{1,0:T(8,128)(2,1)S(1)} %copy-done.3, bf16[2,48,5120]{2,1,0:T(8,128)(2,1)S(1)} %copy-done.1, bf16[2,48,5120]{2,1,0:T(8,128)(2,1)S(1)} %copy-done.2, bf16[1,2,768,640]{3,2,1,0:T(8,128)(2,1)S(1)} %copy-done, s32[2,48,40]{2,1,0:T(8,128)S(1)} %copy.7.exps), custom_call_target="tpu_custom_call" | custom-call | tf_op jit(solution)/shard_map/pallas_call | solution.py:358
  62.3 0.8 %copy.10 = bf16[48,5120]{1,0:T(8,128)(2,1)} copy(bf16[48,5120]{1,0:T(8,128)(2,1)S(1)} %get-tuple-element.4) | data formatting | bytes 983040
  63.0 0.9 %copy.11 = bf16[2,48,5120]{2,1,0:T(8,128)(2,1)} copy(bf16[2,48,5120]{2,1,0:T(8,128)(2,1)S(1)} %get-tuple-element.5) | data formatting | bytes 1966080
Async XLA Ops:
  1.5 1.6 %copy-start = (bf16[1,2,768,640]{3,2,1,0:T(8,128)(2,1)S(1)}, bf16[1,2,768,640]{3,2,1,0:T(8,128)(2,1)}, u32[]{:S(2)}) copy-start(bf16[1,2,768,640]{3,2,1,0:T(8,128)(2,1)} %caches.1) | copy-start | bytes 5898244
  3.0 1.2 %copy-start.1 = (bf16[2,48,5120]{2,1,0:T(8,128)(2,1)S(1)}, bf16[2,48,5120]{2,1,0:T(8,128)(2,1)}, u32[]{:S(2)}) copy-start(bf16[2,48,5120]{2,1,0:T(8,128)(2,1)} %fresh.1) | copy-start | bytes 2949124
  4.2 1.2 %copy-start.2 = (bf16[2,48,5120]{2,1,0:T(8,128)(2,1)S(1)}, bf16[2,48,5120]{2,1,0:T(8,128)(2,1)}, u32[]{:S(2)}) copy-start(bf16[2,48,5120]{2,1,0:T(8,128)(2,1)} %stale.1) | copy-start | bytes 2949124
  5.4 1.0 %copy-start.3 = (bf16[48,5120]{1,0:T(8,128)(2,1)S(1)}, bf16[48,5120]{1,0:T(8,128)(2,1)}, u32[]{:S(2)}) copy-start(bf16[48,5120]{1,0:T(8,128)(2,1)} %query.1) | copy-start | bytes 1474564

commit v2 on v1

--- a/solution.py
+++ b/solution.py
@@ -59,7 +59,7 @@
             ((exps, e_v), (fresh, f_v), (stale, s_v), (query, q_v), (caches, c_v))
         )
     ]
-    for load in loads:
+    for load in loads[:4]:
         load.start()
 
     barrier = pltpu.get_barrier_semaphore()
@@ -124,10 +124,14 @@
         )
 
     loads[0].wait()
-    head_count = e_v.shape[2]
-    lim[...] = (LIMIT * jnp.exp2(e_v[...].astype(jnp.float32))).reshape(2 * rows, head_count).astype(
-        jnp.bfloat16
-    )
+    head_count = e_v.shape[1]
+    turn = lax.broadcasted_iota(jnp.int32, (head_count, head_count), 0)
+    turn = (turn == lax.broadcasted_iota(jnp.int32, (head_count, head_count), 1)).astype(jnp.bfloat16)
+    for which in (0, 1):
+        power = (LIMIT * jnp.exp2(e_v[which].astype(jnp.float32))).astype(jnp.bfloat16)
+        lim[which * rows : (which + 1) * rows] = lax.dot_general(
+            power, turn, (((0,), (0,)), ((), ())), preferred_element_type=jnp.float32
+        ).astype(jnp.bfloat16)
     for load in loads[1:4]:
         load.wait()
 
@@ -157,13 +161,17 @@
                 parts.append(jnp.zeros((spare, head), jnp.float32))
             qsend[s][go * spread + t] = jnp.concatenate(parts, axis=0).astype(jnp.bfloat16)
 
+    for k in ORDER:
+        prepare(0, partner_group(group, k))
+    pl.semaphore_wait(barrier, n - 1)
+    loads[4].start()
+
     for s in range(len(stages)):
         first, count = stages[s]
         for k in ORDER:
             go = partner_group(group, k)
-            prepare(s, go)
-            if s == 0 and k == ORDER[0]:
-                pl.semaphore_wait(barrier, n - 1)
+            if s:
+                prepare(s, go)
             if k:
                 kv_copy(s, go).start()
                 loop(0, spread, lambda t: q_copy(s, go * spread + t).start())
@@ -179,9 +187,14 @@
 
                 loop(0, spread, to_sibling)
 
-    write_renewed = pltpu.make_async_copy(ren, renewed, out_sem.at[0])
+    write_renewed = pltpu.make_async_copy(ren, renewed, in_sem.at[5])
     write_renewed.start()
     loads[4].wait()
+
+    def write_group(s, g):
+        first, count = stages[s]
+        window = pl.ds(pl.multiple_of(g * cols + first * head, 128), count * head)
+        return pltpu.make_async_copy(att.at[:, window], attended.at[:, window], out_sem.at[s, g])
 
     def unpack(s):
         first, count = stages[s]
@@ -201,6 +214,7 @@
                 piece = got[:, j * unit : (j + 1) * unit, :].reshape(spread * unit, head)
                 start = pl.multiple_of(g * cols + (first + j) * head, 128)
                 att[:, pl.ds(start, head)] = join_rows(piece).astype(jnp.bfloat16)
+            write_group(s, g).start()
 
         loop(0, HG, one_group)
 
@@ -281,8 +295,6 @@
 
     for s in range(len(stages)):
         unpack(s)
-    write_attended = pltpu.make_async_copy(att, attended, out_sem.at[1])
-    write_attended.start()
 
     for s in range(len(stages)):
 
@@ -305,7 +317,8 @@
 
         loop(0, spread, left_sibling)
     write_renewed.wait()
-    write_attended.wait()
+    for s in range(len(stages)):
+        loop(0, HG, lambda g: write_group(s, g).wait())
 
 
 def local(query, fresh_kv, own_stale, caches, exponents):
@@ -331,7 +344,7 @@
             pltpu.VMEM(fresh_kv.shape, bf16),
             pltpu.VMEM(own_stale.shape, bf16),
             pltpu.VMEM(caches.shape, bf16),
-            pltpu.VMEM(exponents.shape, jnp.int32),
+            pltpu.VMEM((2, exponents.shape[2], rows), jnp.int32),
             pltpu.VMEM((2 * rows, exponents.shape[2]), bf16),
             pltpu.VMEM((HG, group_heads, 2, rows, head), bf16),
             pltpu.VMEM(query.shape, bf16),
@@ -342,8 +355,8 @@
         + [pltpu.VMEM(pack, bf16) for _ in range(4) for pack in packs]
         + [
             pltpu.VMEM((group_heads, 2, tokens, head), bf16),
-            dma((5,)),
-            dma((2,)),
+            dma((6,)),
+            dma((ns, HG)),
             dma((ns, HG)),
             dma((ns, n)),
             dma((ns, HG, spread)),
@@ -358,16 +371,16 @@
     return pl.pallas_call(
         functools.partial(kernel, sizes),
         out_shape=(
-            jax.ShapeDtypeStruct(query.shape, bf16),
-            jax.ShapeDtypeStruct(fresh_kv.shape, bf16),
+            pltpu.VMEM(query.shape, bf16),
+            pltpu.VMEM(fresh_kv.shape, bf16),
         ),
-        in_specs=[anywhere] * 5,
+        in_specs=[pl.BlockSpec(memory_space=pltpu.HBM)] * 5,
         out_specs=(anywhere, anywhere),
         scratch_shapes=scratch,
         compiler_params=pltpu.CompilerParams(
-            collective_id=0, has_side_effects=True, vmem_limit_bytes=48 * 1024 * 1024
+            collective_id=0, has_side_effects=True, vmem_limit_bytes=60 * 1024 * 1024
         ),
-    )(query, fresh_kv, own_stale, caches, exponents)
+    )(query, fresh_kv, own_stale, caches, exponents.transpose(0, 2, 1))
 
 
 def solution(mesh):

time: 64.3 us -> 57.5 us (0.89)
  local copies, waits for them, and re-layouts: 7.56 us -> 1.72 us
  Pallas kernels: 55.8 us -> 55 us
    unnamed x11 -> x2, local copies, waits for them, and re-layouts: 7.56 us -> 1.72 us
    pallas_call x1, Pallas kernels: 55.8 us -> 55 us  [local(): pl.pallas_call(functools.partial(kernel, sizes), out_shape=(pltpu.VMEM(qu...]
where the time goes in v2:
time: 57.5 us; the launch traced here: 57.4 us
  Pallas kernels  55 us (96%)
  local copies, waits for them, and re-layouts  1.72 us (3%)
  between operations  0.64 us (1%)
    pallas_call x1, Pallas kernels, local(): pl.pallas_call(functools.partial(kernel, sizes), out_shape=(pltpu.VMEM(qu...  55 us
    unnamed x2, local copies, waits for them, and re-layouts  1.72 us

profile of v2, /device:TPU:0, one launch (start us, length us, event | category | flops | bytes accessed | tf_op | source)
XLA Modules:
  0.0 57.4 jit_solution(15693717289037779355)
XLA Ops:
  0.6 55.0 %shard_map.68 = (bf16[48,5120]{1,0:T(8,128)(2,1)S(1)}, bf16[2,48,5120]{2,1,0:T(8,128)(2,1)S(1)}) custom-call(bf16[48,5120]{1,0:T(8,128)(2,1)} %query.1, bf16[2,48,5120]{2,1,0:T(8,128)(2,1)} %fresh.1, bf16[2,48,5120]{2,1,0:T(8,128)(2,1)} %stale.1, bf16[1,2,768,640]{3,2,1,0:T(8,128)(2,1)} %caches.1, s32[2,40,48]{2,1,0:T(8,128)} %bitcast.1), custom_call_target="tpu_custom_call" | custom-call | tf_op jit(solution)/shard_map/pallas_call | solution.py:371
  55.6 0.8 %copy.9 = bf16[48,5120]{1,0:T(8,128)(2,1)} copy(bf16[48,5120]{1,0:T(8,128)(2,1)S(1)} %get-tuple-element.2) | data formatting | bytes 983040
  56.4 0.9 %copy.10 = bf16[2,48,5120]{2,1,0:T(8,128)(2,1)} copy(bf16[2,48,5120]{2,1,0:T(8,128)(2,1)S(1)} %get-tuple-element.3) | data formatting | bytes 1966080

commit v3 on v2

--- a/solution.py
+++ b/solution.py
@@ -41,13 +41,14 @@
 
 def kernel(
     sizes, query, fresh, stale, caches, exps, attended, renewed,
-    q_v, f_v, s_v, c_v, e_v, lim, dec, att, ren, keys, values,
+    q_v, f_v, s_v, c_v, e_v, lim, dec, keys, values,
     qsend0, qsend1, qsend2, qgot0, qgot1, qgot2, osend0, osend1, osend2, ogot0, ogot1, ogot2,
-    arrived, in_sem, out_sem, kv_send, kv_recv, fw_send, q_send, q_recv, o_send, o_recv,
+    arrived0, arrived1, arrived2, in_sem, kv_send, kv_recv, fw_send, q_send, q_recv, o_send, o_recv,
 ):
     n, spread, rows, sub, unit, head, group_heads, stages = sizes
     cols = group_heads * head
     qsend, qgot = (qsend0, qsend1, qsend2), (qgot0, qgot1, qgot2)
+    arrived = (arrived0, arrived1, arrived2)
     osend, ogot = (osend0, osend1, osend2), (ogot0, ogot1, ogot2)
     me = lax.axis_index("patch")
     group, member = lax.div(me, spread), lax.rem(me, spread)
@@ -77,12 +78,8 @@
             device_id={"patch": device}, device_id_type=MESH,
         )
 
-    def slab_rows(p):
-        return pl.ds(pl.multiple_of(p * rows, 16), rows)
-
     def landed(s, p):
-        first, count = stages[s]
-        return arrived.at[pl.ds(first, count), :, slab_rows(p), :]
+        return arrived[s].at[p]
 
     def kv_copy(s, go):
         first, count = stages[s]
@@ -150,7 +147,7 @@
         decoded = jnp.clip(residual, -limit, limit).astype(jnp.bfloat16)
         for j in range(count):
             dec[go, first + j] = decoded[:, :, j * head : (j + 1) * head]
-        ren[:, :, window] = (old + decoded.astype(jnp.float32)).astype(jnp.bfloat16)
+        renewed[:, :, window] = (old + decoded.astype(jnp.float32)).astype(jnp.bfloat16)
         block = spread_rows(q_v[:, window].astype(jnp.float32))
         for t in range(spread):
             parts = [
@@ -176,7 +173,7 @@
                 kv_copy(s, go).start()
                 loop(0, spread, lambda t: q_copy(s, go * spread + t).start())
             else:
-                arrived[pl.ds(first, count), :, my_rows, :] = dec[group, pl.ds(first, count)]
+                arrived[s][me] = dec[group, pl.ds(first, count)]
                 qgot[s][me] = qsend[s][me]
 
                 def to_sibling(t):
@@ -187,14 +184,7 @@
 
                 loop(0, spread, to_sibling)
 
-    write_renewed = pltpu.make_async_copy(ren, renewed, in_sem.at[5])
-    write_renewed.start()
     loads[4].wait()
-
-    def write_group(s, g):
-        first, count = stages[s]
-        window = pl.ds(pl.multiple_of(g * cols + first * head, 128), count * head)
-        return pltpu.make_async_copy(att.at[:, window], attended.at[:, window], out_sem.at[s, g])
 
     def unpack(s):
         first, count = stages[s]
@@ -213,10 +203,18 @@
             for j in range(count):
                 piece = got[:, j * unit : (j + 1) * unit, :].reshape(spread * unit, head)
                 start = pl.multiple_of(g * cols + (first + j) * head, 128)
-                att[:, pl.ds(start, head)] = join_rows(piece).astype(jnp.bfloat16)
-            write_group(s, g).start()
+                attended[:, pl.ds(start, head)] = join_rows(piece).astype(jnp.bfloat16)
 
         loop(0, HG, one_group)
+
+    def give_back(s, p):
+        @pl.when(p != me)
+        def _():
+            o_copy(s, p).start()
+
+        @pl.when(p == me)
+        def _():
+            ogot[s][me] = osend[s][me]
 
     scale = head ** (-0.5) * math.log2(math.e)
     chunk = 8
@@ -255,7 +253,7 @@
             for which, store in ((0, keys), (1, values)):
                 store[j] = (
                     c_v[0, which, :, columns].astype(jnp.float32)
-                    + arrived[first + j, which].astype(jnp.float32)
+                    + arrived[s][:, j, which].reshape(n * rows, head).astype(jnp.float32)
                 ).astype(jnp.bfloat16)
                 store[j, my_rows, :] = f_v[which, :, mine]
 
@@ -280,18 +278,7 @@
                 outs.append(jnp.zeros((chunk, spare, head), jnp.float32))
             osend[s][c0 : c0 + chunk] = jnp.concatenate(outs, axis=1).astype(jnp.bfloat16)
 
-            def give_back(i):
-                p = c0 + i
-
-                @pl.when(p != me)
-                def _():
-                    o_copy(s, p).start()
-
-                @pl.when(p == me)
-                def _():
-                    ogot[s][me] = osend[s][me]
-
-            loop(0, chunk, give_back)
+            loop(c0, c0 + chunk, lambda p: give_back(s, p))
 
     for s in range(len(stages)):
         unpack(s)
@@ -316,9 +303,6 @@
                 loop(0, HG, one)
 
         loop(0, spread, left_sibling)
-    write_renewed.wait()
-    for s in range(len(stages)):
-        loop(0, HG, lambda g: write_group(s, g).wait())
 
 
 def local(query, fresh_kv, own_stale, caches, exponents):
@@ -330,7 +314,7 @@
     group_heads = exponents.shape[2] // HG
     cols = width // HG
     unit = round_up(sub, 8)
-    cuts = (0, 2, 4, group_heads)
+    cuts = (0, 1, 3, group_heads)
     stages = tuple((a, b - a) for a, b in zip(cuts[:-1], cuts[1:]))
     tokens = caches.shape[2]
     most = max(count for _, count in stages)
@@ -347,16 +331,13 @@
             pltpu.VMEM((2, exponents.shape[2], rows), jnp.int32),
             pltpu.VMEM((2 * rows, exponents.shape[2]), bf16),
             pltpu.VMEM((HG, group_heads, 2, rows, head), bf16),
-            pltpu.VMEM(query.shape, bf16),
-            pltpu.VMEM(fresh_kv.shape, bf16),
             pltpu.VMEM((most, tokens, head), bf16),
             pltpu.VMEM((most, tokens, head), bf16),
         ]
         + [pltpu.VMEM(pack, bf16) for _ in range(4) for pack in packs]
+        + [pltpu.VMEM((n, count, 2, rows, head), bf16) for _, count in stages]
         + [
-            pltpu.VMEM((group_heads, 2, tokens, head), bf16),
-            dma((6,)),
-            dma((ns, HG)),
+            dma((5,)),
             dma((ns, HG)),
             dma((ns, n)),
             dma((ns, HG, spread)),
@@ -375,7 +356,7 @@
             pltpu.VMEM(fresh_kv.shape, bf16),
         ),
         in_specs=[pl.BlockSpec(memory_space=pltpu.HBM)] * 5,
-        out_specs=(anywhere, anywhere),
+        out_specs=(pl.BlockSpec(memory_space=pltpu.VMEM),) * 2,
         scratch_shapes=scratch,
         compiler_params=pltpu.CompilerParams(
             collective_id=0, has_side_effects=True, vmem_limit_bytes=60 * 1024 * 1024

time: 57.5 us -> 56.9 us (0.990)
  Pallas kernels: 55 us -> 54.4 us
    pallas_call x1, Pallas kernels: 55 us -> 54.4 us  [local(): pl.pallas_call(functools.partial(kernel, sizes), out_shape=(pltpu.VMEM(qu...]
where the time goes in v3:
time: 56.9 us; the launch traced here: 56.7 us
  Pallas kernels  54.4 us (96%)
  local copies, waits for them, and re-layouts  1.72 us (3%)
  between operations  0.64 us (1%)
    pallas_call x1, Pallas kernels, local(): pl.pallas_call(functools.partial(kernel, sizes), out_shape=(pltpu.VMEM(qu...  54.4 us
    unnamed x2, local copies, waits for them, and re-layouts  1.72 us

profile of v3, /device:TPU:0, one launch (start us, length us, event | category | flops | bytes accessed | tf_op | source)
XLA Modules:
  0.0 56.7 jit_solution(17901567921287063160)
XLA Ops:
  0.6 54.4 %shard_map.68 = (bf16[48,5120]{1,0:T(8,128)(2,1)S(1)}, bf16[2,48,5120]{2,1,0:T(8,128)(2,1)S(1)}) custom-call(bf16[48,5120]{1,0:T(8,128)(2,1)} %query.1, bf16[2,48,5120]{2,1,0:T(8,128)(2,1)} %fresh.1, bf16[2,48,5120]{2,1,0:T(8,128)(2,1)} %stale.1, bf16[1,2,768,640]{3,2,1,0:T(8,128)(2,1)} %caches.1, s32[2,40,48]{2,1,0:T(8,128)} %bitcast.1), custom_call_target="tpu_custom_call" | custom-call | tf_op jit(solution)/shard_map/pallas_call | solution.py:352
  55.0 0.8 %copy.9 = bf16[48,5120]{1,0:T(8,128)(2,1)} copy(bf16[48,5120]{1,0:T(8,128)(2,1)S(1)} %get-tuple-element.2) | data formatting | bytes 983040
  55.8 0.9 %copy.10 = bf16[2,48,5120]{2,1,0:T(8,128)(2,1)} copy(bf16[2,48,5120]{2,1,0:T(8,128)(2,1)S(1)} %get-tuple-element.3) | data formatting | bytes 1966080
